TPU v7x, 128 devices: a whole 4x4x4 slice. The times are simulated.
128 devices in a mesh: row: 8 (over x, y_lo), col: 16 (over z, y_hi, core).
Axes of the slice: x: 4, y: 4 (y_hi: 2, y_lo: 2; y = y_hi * 2 + y_lo), z: 4, core: 2. Of those that a mesh axis runs over, the one named last changes fastest.
Arguments:
- halves: float32 [2, 4096, 16384], P(None, 'row', 'col'), may hold values from -6 to 6
- diag_rest: float32 [8192, 1024], P(('col', 'row')), may hold values from -6 to 6
- panel_vectors: float32 [16384, 256], P('col'), may hold values from -1 to 1
- tri_factor: float32 [256, 256], replicated, may hold values from -1 to 2, as said below
Outputs:
- updated_halves: float32 [2, 4096, 16384], P(None, 'row', 'col')
- updated_rest: float32 [8192, 1024], P(('col', 'row'))
- w_panel: float32 [16384, 256], P('col')
Inputs may be any that keep to these rules, and one draw needn't show every extreme that they name: `tri_factor`: upper triangular, diagonal between 1 and 2.
All inputs are finite; a program needn't handle non-finite values.
Results may differ from a plain program's by a relative error of at most 0.0003.
Values sent between devices are 32-bit elements; how exact they have to be, the bound alone decides.
A program may use at most 64 MiB of HBM per device.

v0:
```python
import jax
import jax.numpy as jnp
from jax import lax
from jax.sharding import PartitionSpec as P

precise = lax.Precision.HIGHEST


def broadcast(value, axis, source):
    kept = jnp.where(lax.axis_index(axis) == source, value, 0).astype(value.dtype)
    return lax.psum(kept, axis)


def matmul(left, right):
    return jnp.dot(left, right, precision=precise, preferred_element_type=jnp.float32)


def left_contract(left, right):
    return lax.dot_general(
        left, right, (((0,), (0,)), ((), ())), precision=precise, preferred_element_type=jnp.float32
    )


def right_contract(left, right):
    return lax.dot_general(
        left, right, (((1,), (1,)), ((), ())), precision=precise, preferred_element_type=jnp.float32
    )


def shards(halves, diag_rest, panel_vectors, tri_factor):
    row_count = lax.axis_size("row")
    row_index = lax.axis_index("row")
    col_index = lax.axis_index("col")
    half_size = halves.shape[1]
    tile_size = halves.shape[2]
    panel_width = panel_vectors.shape[1]
    rest_rows = diag_rest.shape[0]
    rest_start = half_size + row_index * rest_rows
    zero_block = jnp.zeros((tile_size, panel_width), jnp.float32)
    row_vecs = []
    for position in range(2):
        row_vecs.append(broadcast(panel_vectors, "col", row_index + row_count * position))
    layout = []
    row_parts = []
    col_part = zero_block
    for position in range(2):
        block_row = row_index + row_count * position
        is_lower = block_row >= col_index
        weight = jnp.where(block_row == col_index, 0.5, 1.0).astype(jnp.float32)
        offset = jnp.where(is_lower, 0, half_size).astype(jnp.int32)
        low_vec = jnp.where(is_lower, panel_vectors, row_vecs[position])
        high_vec = jnp.where(is_lower, row_vecs[position], panel_vectors)
        high_half = lax.dynamic_slice_in_dim(high_vec, offset, half_size, 0)
        first = matmul(halves[position], low_vec) * weight
        second = left_contract(halves[position], high_half) * weight
        padded = lax.dynamic_update_slice_in_dim(zero_block, first, offset, 0)
        row_parts.append(jnp.where(is_lower, padded, second))
        col_part = col_part + jnp.where(is_lower, second, padded)
        layout.append((block_row, is_lower, offset, low_vec, high_half))
    own_rest_vec = lax.dynamic_slice_in_dim(panel_vectors, rest_start, rest_rows, 0)
    rest_first = lax.dynamic_update_slice_in_dim(
        zero_block, matmul(diag_rest, panel_vectors), rest_start, 0
    )
    col_part = col_part + 0.5 * (rest_first + left_contract(diag_rest, own_rest_vec))
    row_totals = lax.psum(jnp.stack(row_parts), "col")
    extra = zero_block
    for position in range(2):
        block_row = row_index + row_count * position
        extra = extra + jnp.where(block_row == col_index, row_totals[position], 0.0)
    col_terms = col_part + extra
    av_block = lax.psum(col_terms, "row")
    inner = lax.psum(left_contract(panel_vectors, av_block), "col")
    middle = matmul(left_contract(tri_factor, inner), tri_factor)
    w_own = matmul(av_block, tri_factor) - 0.5 * matmul(panel_vectors, middle)
    row_ws = []
    for position in range(2):
        row_ws.append(broadcast(w_own, "col", row_index + row_count * position))
    updated = []
    for position in range(2):
        block_row, is_lower, offset, low_vec, high_half = layout[position]
        low_w = jnp.where(is_lower, w_own, row_ws[position])
        high_w = jnp.where(is_lower, row_ws[position], w_own)
        high_whalf = lax.dynamic_slice_in_dim(high_w, offset, half_size, 0)
        left = jnp.concatenate([high_half, high_whalf], 1)
        right = jnp.concatenate([low_w, low_vec], 1)
        updated.append(halves[position] - right_contract(left, right))
    own_rest_w = lax.dynamic_slice_in_dim(w_own, rest_start, rest_rows, 0)
    left_rest = jnp.concatenate([own_rest_vec, own_rest_w], 1)
    right_rest = jnp.concatenate([w_own, panel_vectors], 1)
    new_rest = diag_rest - right_contract(left_rest, right_rest)
    return (jnp.stack(updated), new_rest, w_own)


def solution(mesh):
    return jax.shard_map(
        shards,
        mesh=mesh,
        in_specs=(P(None, "row", "col"), P(("col", "row"), None), P("col", None), P()),
        out_specs=(P(None, "row", "col"), P(("col", "row"), None), P("col", None)),
        check_vma=False,
    )
```

profile of v0, /device:TPU:0, one launch (start us, length us, event | category | flops | bytes accessed | tf_op | source)
XLA Modules:
  0.0 716.4 jit_solution(4993959610792432966)
XLA Ops:
  7.2 0.0 copy-start
  7.2 0.0 all-reduce.16.cloned.1.call-start
  7.2 1.6 copy.7
  8.8 1.6 broadcast_select_fusion.3
  10.5 0.0 all-reduce.16.cloned.1.call-update
  10.5 0.0 all-reduce.8.cloned.1.call-start
  10.6 149.7 %all-reduce.16.cloned.1.call-done = (f32[1024,256]{0,1:T(8,128)}, f32[1024,256]{0,1:T(8,128)}) async-done(((f32[1024,256]{0,1:T(8,128)}, f32[1024,256]{0,1:T(8,128)}), (f32[1024,256]{0,1:T(8,128)}, f32[1024,256]{0,1:T(8,128)})) %all-reduce.16.cloned.1.call-update) | async-done | bytes 2097168 | tf_op jit(solution)/shard_map/psum | solution.py:11
  160.3 0.3 broadcast_select_fusion.6
  160.6 0.9 copy-done.18
  161.5 2.3 dynamic-slice_select_fusion.3
  163.8 0.0 copy-start.12
  163.8 0.0 copy-start.14
  163.9 1.9 fusion.35
  165.8 1.9 fusion.41
  167.7 0.1 broadcast_in_dim.13.clone.1
  167.9 1.9 fusion.50
  169.8 0.1 broadcast_in_dim.13.clone
  170.0 1.9 fusion.59
  171.9 0.0 copy-done.9
  171.9 0.0 copy-done.10
  171.9 0.0 copy-done.4
  171.9 0.4 select_bitcast_fusion
  172.3 1.5 pad_maximum_fusion.1
  173.8 0.0 all-reduce.8.cloned.1.call-update
  173.8 0.2 all-reduce.10.cloned.1.call-start
  174.0 0.1 constant_dynamic-slice_fusion.1
  174.2 1.9 fusion.80
  176.1 0.0 copy-start.11
  176.1 1.0 copy-done.11
  177.1 3.4 convolution_add_fusion
  180.5 1.8 add.59
  182.2 138.8 %all-reduce.8.cloned.1.call-done = f32[2,1024,256]{1,2,0:T(8,128)} async-done(((f32[2,1024,256]{1,2,0:T(8,128)}), f32[2,1024,256]{1,2,0:T(8,128)}) %all-reduce.8.cloned.1.call-update) | async-done | bytes 2097168 | tf_op jit(solution)/shard_map/psum | solution.py:65
  321.0 4.3 fusion.67
  325.3 0.0 all-reduce.10.cloned.1.call-update
  325.3 0.0 all-reduce.12.cloned.1.call-start
  325.4 77.6 %all-reduce.10.cloned.1.call-done = f32[1024,256]{0,1:T(8,128)} async-done(((f32[1024,256]{0,1:T(8,128)}), f32[1024,256]{0,1:T(8,128)}) %all-reduce.10.cloned.1.call-update) | async-done | bytes 1048592 | tf_op jit(solution)/shard_map/psum | solution.py:71
  403.0 3.0 convolution_bitcast_fusion
  406.0 0.0 all-reduce.12.cloned.1.call-update
  406.1 0.0 all-reduce.14.cloned.1.call-start
  406.1 0.0 copy-done
  406.1 0.0 copy-done.16
  406.1 2.1 fusion.81
  408.2 134.5 %all-reduce.12.cloned.1.call-done = f32[256,256]{0,1:T(8,128)} async-done(((f32[256,256]{0,1:T(8,128)}), f32[256,256]{0,1:T(8,128)}) %all-reduce.12.cloned.1.call-update) | async-done | bytes 262160 | tf_op jit(solution)/shard_map/psum | solution.py:72
  542.7 1.4 fusion.82
  544.2 0.6 fusion.83
  544.8 3.3 broadcast_select_fusion.1
  548.1 0.0 all-reduce.14.cloned.1.call-update
  548.1 1.3 copy.17
  549.4 0.1 constant_dynamic-slice_fusion
  549.6 0.0 copy-done.21
  549.6 2.1 fusion.62
  551.7 144.4 %all-reduce.14.cloned.1.call-done = (f32[1024,256]{0,1:T(8,128)}, f32[1024,256]{0,1:T(8,128)}) async-done(((f32[1024,256]{0,1:T(8,128)}, f32[1024,256]{0,1:T(8,128)}), (f32[1024,256]{0,1:T(8,128)}, f32[1024,256]{0,1:T(8,128)})) %all-reduce.14.cloned.1.call-update) | async-done | bytes 2097168 | tf_op jit(solution)/shard_map/psum | solution.py:11
  696.1 1.6 dynamic-slice_select_fusion.1
  697.6 0.0 copy-done.19
  697.6 0.3 copy-done.20
  697.9 0.3 broadcast_select_fusion.7
  698.2 0.0 copy-done.15
  698.2 1.9 copy-done.2
  700.1 0.3 copy-done.8
  700.4 3.5 fusion.21
  704.0 0.0 copy-done.6
  704.0 0.0 copy-done.13
  704.0 3.6 fusion.16
  707.6 2.3 pad_maximum_fusion
  (25 shorter events, 0.0 us)
Async XLA Ops:
  7.2 399.0 %copy-start = (f32[256,256]{1,0:T(8,128)S(1)}, f32[256,256]{1,0:T(8,128)}, u32[]{:S(2)}) copy-start(f32[256,256]{1,0:T(8,128)} %param.7) | copy-start | bytes 786436
  7.2 153.1 %all-reduce.16.cloned.1.call-start = ((), (), s32[]{:S(2)}) async-start(), calls=%async_computation.4 | async-start | bytes 4194304 | tf_op jit(solution)/shard_map/psum | solution.py:11
  10.5 310.5 %all-reduce.8.cloned.1.call-start = ((), (), s32[]{:S(2)}) async-start(), calls=%async_computation | async-start | bytes 4194304 | tf_op jit(solution)/shard_map/psum | solution.py:65
  160.3 1.2 copy-start.18
  160.3 3.6 copy-start.1
  161.5 6.4 copy-start.7
  161.5 8.4 %copy-start.5 = (f32[1024,256]{0,1:T(8,128)}, f32[1024,256]{0,1:T(8,128)S(1)}, u32[]{:S(2)}) copy-start(f32[1024,256]{0,1:T(8,128)S(1)} %get-tuple-element.19) | copy-start | bytes 3145732
  163.8 3.9 copy-start.12
  163.8 3.9 copy-start.14
  165.8 6.1 copy-start.9
  167.7 4.2 copy-start.10
  169.8 2.1 copy-start.4
  173.8 3.3 copy-start.3
  173.8 229.2 %all-reduce.10.cloned.1.call-start = ((), (), s32[]{:S(2)}) async-start(), calls=%async_computation.1 | async-start | bytes 2097152 | tf_op jit(solution)/shard_map/psum | solution.py:71
  176.1 1.0 copy-start.11
  325.3 217.4 %all-reduce.12.cloned.1.call-start = ((), (), s32[]{:S(2)}) async-start(), calls=%async_computation.2 | async-start | bytes 524288 | tf_op jit(solution)/shard_map/psum | solution.py:72
  403.0 3.1 copy-start.16
  406.1 290.0 %all-reduce.14.cloned.1.call-start = ((), (), s32[]{:S(2)}) async-start(), calls=%async_computation.3 | async-start | bytes 4194304 | tf_op jit(solution)/shard_map/psum | solution.py:11
  542.7 2.0 copy-start.17
  548.1 1.4 copy-start.21
  696.1 1.6 copy-start.19
  696.1 1.9 copy-start.20
  696.1 2.1 copy-start.15
  697.9 2.2 copy-start.2
  697.9 2.5 copy-start.8
  700.4 3.5 copy-start.6
  700.4 3.6 copy-start.13
Sparse Core Ops, SparseCore 0:
  11.1 149.0 all-reduce.15
  173.9 147.0 all-reduce.7
  325.5 77.5 all-reduce.9
  406.2 136.5 all-reduce.11
  548.3 147.7 all-reduce.13
where the time goes:
time: 717 us; the launch traced here: 716 us
  waiting for transfers between devices  645 us (90%)
  matrix products  32.7 us (5%)
  other arithmetic  14.6 us (2%)
  between operations  14.1 us (2%)
  local copies, waits for them, and re-layouts  9.56 us (1%)
    psum x2, waiting for transfers between devices, broadcast(): return lax.psum(kept, axis)  294 us
    psum x1, waiting for transfers between devices, shards(): row_totals = lax.psum(jnp.stack(row_parts), 'col')  139 us
    psum x1, waiting for transfers between devices, shards(): inner = lax.psum(left_contract(panel_vectors, av_block), 'col')  135 us
    psum x1, waiting for transfers between devices, shards(): av_block = lax.psum(col_terms, 'row')  77.6 us
  transfers between devices with their start and end apart: 5, of which 5 were waited for; matrix products, arithmetic and copies ran while one was open for 2% of the time, Pallas kernels for 0%

commit v1 on v0

--- a/solution.py
+++ b/solution.py
@@ -1,9 +1,17 @@
+import functools
 import jax
 import jax.numpy as jnp
 from jax import lax
 from jax.sharding import PartitionSpec as P
 
 precise = lax.Precision.HIGHEST
+
+
+def squares_number(matrix, axis_tag):
+    return jnp.sum(lax.all_gather(matrix, axis_name=axis_tag), 0)
+
+
+number_the_cells = functools.partial(squares_number, axis_tag="col")
 
 
 def broadcast(value, axis, source):
@@ -62,7 +70,7 @@
         zero_block, matmul(diag_rest, panel_vectors), rest_start, 0
     )
     col_part = col_part + 0.5 * (rest_first + left_contract(diag_rest, own_rest_vec))
-    row_totals = lax.psum(jnp.stack(row_parts), "col")
+    row_totals = number_the_cells(jnp.stack(row_parts))
     extra = zero_block
     for position in range(2):
         block_row = row_index + row_count * position

time: 717 us -> 778 us (1.085)
  waiting for transfers between devices: 645 us -> 682 us
  other arithmetic: 14.6 us -> 27.6 us
  local copies, waits for them, and re-layouts: 9.56 us -> 21.1 us
    all_gather x0 -> x1, waiting for transfers between devices: none -> 179 us  [squares_number(): return jnp.sum(lax.all_gather(matrix, axis_name=axis_tag), 0)]
    psum x1 -> x0, waiting for transfers between devices: 139 us -> none  [shards(): row_totals = lax.psum(jnp.stack(row_parts), 'col')]
    reduce_sum x0 -> x1, other arithmetic: none -> 13.4 us  [squares_number(): return jnp.sum(lax.all_gather(matrix, axis_name=axis_tag), 0)]
where the time goes in v1:
time: 778 us
  waiting for transfers between devices  682 us (88%)
  matrix products  32.7 us (4%)
  other arithmetic  27.6 us (4%)
  local copies, waits for them, and re-layouts  21.1 us (3%)
  between operations  14.1 us (2%)
    psum x2, waiting for transfers between devices, broadcast(): return lax.psum(kept, axis)  294 us
    all_gather x1, waiting for transfers between devices, squares_number(): return jnp.sum(lax.all_gather(matrix, axis_name=axis_tag), 0)  179 us
    psum x1, waiting for transfers between devices, shards(): inner = lax.psum(left_contract(panel_vectors, av_block), 'col')  135 us
    psum x1, waiting for transfers between devices, shards(): av_block = lax.psum(col_terms, 'row')  74.7 us
  transfers between devices with their start and end apart: 5, of which 5 were waited for; matrix products, arithmetic and copies ran while one was open for 2% of the time, Pallas kernels for 0%

profile of v1, /device:TPU:0, one launch (start us, length us, event | category | flops | bytes accessed | tf_op | source)
XLA Modules:
  0.0 777.7 jit_solution(10325205442690874482)
XLA Ops:
  7.2 0.0 copy-start
  7.2 0.0 all-reduce.13.cloned.1.call-start
  7.2 1.6 copy.30
  8.8 1.6 broadcast_select_fusion.3
  10.5 0.0 all-reduce.13.cloned.1.call-update
  10.5 0.0 all-gather.3.cloned.1.call-start
  10.6 149.7 %all-reduce.13.cloned.1.call-done = (f32[1024,256]{0,1:T(8,128)}, f32[1024,256]{0,1:T(8,128)}) async-done(((f32[1024,256]{0,1:T(8,128)}, f32[1024,256]{0,1:T(8,128)}), (f32[1024,256]{0,1:T(8,128)}, f32[1024,256]{0,1:T(8,128)})) %all-reduce.13.cloned.1.call-update) | async-done | bytes 2097168 | tf_op jit(solution)/shard_map/psum | solution.py:19
  160.3 0.3 broadcast_select_fusion.6
  160.6 0.9 copy-done.18
  161.5 2.3 dynamic-slice_select_fusion.3
  163.8 0.0 copy-start.12
  163.8 0.0 copy-start.14
  163.9 0.0 copy-done.1
  163.9 1.9 fusion.35
  165.8 0.0 copy-start.9
  165.8 1.9 fusion.41
  167.7 0.1 broadcast_in_dim.13.clone.1
  167.9 1.9 fusion.50
  169.8 0.1 broadcast_in_dim.13.clone
  169.9 1.9 fusion.59
  171.9 0.0 copy-done.9
  171.9 0.0 copy-done.10
  171.9 0.0 copy-start.4
  171.9 0.4 select_bitcast_fusion
  172.3 0.6 copy-done.4
  172.9 1.5 pad_maximum_fusion.1
  174.4 2.9 copy.38
  177.2 0.0 all-gather.3.cloned.1.call-update
  177.3 0.2 all-reduce.7.cloned.1.call-start
  177.5 0.1 constant_dynamic-slice_fusion.1
  177.6 1.9 fusion.78
  179.5 1.0 copy-done.11
  180.6 3.4 convolution_add_fusion
  184.0 1.8 add.57
  185.8 178.5 %all-gather.3.cloned.1.call-done = f32[32,1024,256]{2,1,0:T(8,128)} async-done(((f32[2,1024,256]{2,1,0:T(8,128)}), f32[32,1024,256]{2,1,0:T(8,128)}) %all-gather.3.cloned.1.call-update) | async-done | bytes 33554448 | tf_op jit(solution)/shard_map/all_gather | solution.py:11
  364.3 13.4 %reduce_sum.9 = f32[2,1024,256]{2,1,0:T(8,128)} reduce(f32[16,2,1024,256]{3,2,1,0:T(8,128)} %bitcast.86, f32[]{:T(128)} %constant.8.clone.1), dimensions={0}, to_apply=%region_2.3 | reduce | flops 7864320 | bytes 35651588 | tf_op jit(solution)/shard_map/reduce_sum | solution.py:11
  377.7 3.0 fusion.77
  380.7 2.5 copy.46
  383.2 2.5 copy.47
  385.7 4.0 bitcast_add_fusion
  389.7 0.0 all-reduce.7.cloned.1.call-update
  389.8 0.0 all-reduce.9.cloned.1.call-start
  389.8 74.7 %all-reduce.7.cloned.1.call-done = f32[1024,256]{0,1:T(8,128)} async-done(((f32[1024,256]{0,1:T(8,128)}), f32[1024,256]{0,1:T(8,128)}) %all-reduce.7.cloned.1.call-update) | async-done | bytes 1048592 | tf_op jit(solution)/shard_map/psum | solution.py:79
  464.5 3.0 convolution_bitcast_fusion
  467.6 0.0 all-reduce.9.cloned.1.call-update
  467.6 0.0 all-reduce.11.cloned.1.call-start
  467.6 2.1 fusion.79
  469.7 134.5 %all-reduce.9.cloned.1.call-done = f32[256,256]{0,1:T(8,128)} async-done(((f32[256,256]{0,1:T(8,128)}), f32[256,256]{0,1:T(8,128)}) %all-reduce.9.cloned.1.call-update) | async-done | bytes 262160 | tf_op jit(solution)/shard_map/psum | solution.py:80
  604.2 1.4 fusion.80
  605.7 0.6 fusion.81
  606.3 3.3 broadcast_select_fusion.1
  609.6 0.0 all-reduce.11.cloned.1.call-update
  609.6 1.3 copy.43
  610.9 0.1 constant_dynamic-slice_fusion
  611.0 2.1 fusion.62
  613.2 144.1 %all-reduce.11.cloned.1.call-done = (f32[1024,256]{0,1:T(8,128)}, f32[1024,256]{0,1:T(8,128)}) async-done(((f32[1024,256]{0,1:T(8,128)}, f32[1024,256]{0,1:T(8,128)}), (f32[1024,256]{0,1:T(8,128)}, f32[1024,256]{0,1:T(8,128)})) %all-reduce.11.cloned.1.call-update) | async-done | bytes 2097168 | tf_op jit(solution)/shard_map/psum | solution.py:19
  757.3 1.6 dynamic-slice_select_fusion.1
  758.8 0.3 copy-done.20
  759.1 0.3 broadcast_select_fusion.7
  759.4 1.9 copy-done.2
  761.3 0.3 copy-done.8
  761.6 3.6 fusion.21
  765.2 3.6 fusion.16
  768.8 2.3 pad_maximum_fusion
  (30 shorter events, 0.1 us)
Async XLA Ops:
  7.2 460.5 %copy-start = (f32[256,256]{1,0:T(8,128)S(1)}, f32[256,256]{1,0:T(8,128)}, u32[]{:S(2)}) copy-start(f32[256,256]{1,0:T(8,128)} %param.7) | copy-start | bytes 786436
  7.2 153.1 %all-reduce.13.cloned.1.call-start = ((), (), s32[]{:S(2)}) async-start(), calls=%async_computation.4 | async-start | bytes 4194304 | tf_op jit(solution)/shard_map/psum | solution.py:19
  10.5 353.8 %all-gather.3.cloned.1.call-start = ((), (), s32[]{:S(2)}) async-start(), calls=%async_computation.2 | async-start | bytes 35651584 | tf_op jit(solution)/shard_map/all_gather | solution.py:11
  160.3 1.2 copy-start.18
  160.3 3.6 copy-start.1
  161.5 6.4 copy-start.7
  161.5 8.4 %copy-start.5 = (f32[1024,256]{0,1:T(8,128)}, f32[1024,256]{0,1:T(8,128)S(1)}, u32[]{:S(2)}) copy-start(f32[1024,256]{0,1:T(8,128)S(1)} %get-tuple-element.27) | copy-start | bytes 3145732
  163.8 3.9 copy-start.12
  163.8 3.9 copy-start.14
  165.8 6.1 copy-start.9
  167.7 4.2 copy-start.10
  171.9 1.0 copy-start.4
  177.2 3.3 copy-start.3
  177.3 287.2 %all-reduce.7.cloned.1.call-start = ((), (), s32[]{:S(2)}) async-start(), calls=%async_computation | async-start | bytes 2097152 | tf_op jit(solution)/shard_map/psum | solution.py:79
  179.5 1.0 copy-start.11
  389.8 214.5 %all-reduce.9.cloned.1.call-start = ((), (), s32[]{:S(2)}) async-start(), calls=%async_computation.1 | async-start | bytes 524288 | tf_op jit(solution)/shard_map/psum | solution.py:80
  464.5 3.1 copy-start.16
  467.6 289.7 %all-reduce.11.cloned.1.call-start = ((), (), s32[]{:S(2)}) async-start(), calls=%async_computation.3 | async-start | bytes 4194304 | tf_op jit(solution)/shard_map/psum | solution.py:19
  604.2 2.0 copy-start.17
  609.6 1.4 copy-start.21
  757.3 1.6 copy-start.19
  757.3 1.9 copy-start.20
  757.3 2.1 copy-start.15
  759.1 2.2 copy-start.2
  759.1 2.5 copy-start.8
  761.6 3.6 copy-start.6
  761.6 3.6 copy-start.13
Sparse Core Ops, SparseCore 0:
  11.1 149.0 all-reduce.12
  177.4 186.8 all-gather.2
  389.9 74.5 all-reduce.6
  467.7 136.5 all-reduce.8
  609.7 147.4 all-reduce.10
